TPU v7x, 32 devices: a whole 2x2x4 slice. The times are simulated.
32 devices in a mesh: frames: 2 (over y), row: 4 (over x, core), col: 4 (over z).
Axes of the slice: x: 2, y: 2, z: 4, core: 2. Of those that a mesh axis runs over, the one named last changes fastest.
Arguments:
- mask_pixels: int32 [2048, 2048], P(('frames', 'row'), 'col'), parts along dimension 0, may hold values 0 or 1
- across_taps: bfloat16 [12, 2, 33], replicated, may hold values from -1 to 1
- down_taps: bfloat16 [12, 2, 33], replicated, may hold values from -1 to 1
- kernel_weights: float32 [12], replicated, may hold values from 0.05 to 0.5
- library: bfloat16 [32, 64, 128], P('col'), may hold values from 0 to 4
- cell_ids: int32 [8, 4, 8], P(('frames', 'row'), 'col'), parts along dimension 0, may hold values from 0 to 31, as said below
- cell_slots: int32 [8, 4, 8], P(('frames', 'row'), 'col'), parts along dimension 0, may hold values from 0 to 15, as said below
- cell_count: int32 [8, 4], P(('frames', 'row'), 'col'), parts along dimension 0, may hold values from 2 to 8
Outputs:
- resist: float32 [2048, 2048], P(('frames', 'row'), 'col'), parts along dimension 0
There are 2 independent parts, one for each index of `frames`. A program takes and returns all parts, laid end to end along the dimension named above; an argument that names none is the same for every part. Nothing has to cross between parts.
Inputs may be any that keep to these rules, and one draw needn't show every extreme that they name: `cell_ids`: among the 8 entries of a tile's list, at most 2 name cells of one block of 8 consecutive ids (k * 8 to k * 8 + 7), and the first two entries name cells of one such block. `cell_slots`: the slots of a tile's list are distinct.
All inputs are finite; a program needn't handle non-finite values. No bound on the sum of `mask_pixels` on one device may be relied on, other than what follows from the above.
Results may differ from a plain program's by a relative error of at most 0.00045.
Values may be sent and summed in bfloat16 or wider, within the bound.
A program may use at most 64 MiB of HBM per device.

v0:
```python
import jax
import jax.numpy as jnp
from jax import lax
from jax.sharding import PartitionSpec as P

BLUR_HALF = 8
BLUR_SIGMA = 4.0


def extended_2(x, sides, width):
    for axis, dim in sides:
        count, length = (lax.axis_size(axis), x.shape[dim])
        up = [(i, (i + 1) % count) for i in range(count - 1)]
        down = [(j, i) for i, j in up]
        last = lax.slice_in_dim(x, length - width, length, axis=dim)
        initial = lax.slice_in_dim(x, 0, width, axis=dim)
        before = lax.ppermute(last, axis, up)
        after = lax.ppermute(initial, axis, down)
        x = jnp.concatenate([before, x, after], axis=dim)
    return x


def band_matrix(tap_values, half_width):
    window = 128 + 2 * half_width
    grid_shape = (window, 128, 2 * half_width + 1)
    in_index = lax.broadcasted_iota(jnp.int32, grid_shape, 0)
    out_index = lax.broadcasted_iota(jnp.int32, grid_shape, 1)
    lag_index = lax.broadcasted_iota(jnp.int32, grid_shape, 2)
    picker = (in_index - out_index == lag_index).astype(tap_values.dtype)
    return jnp.einsum(
        "...t,ijt->...ij",
        tap_values,
        picker,
        preferred_element_type=jnp.float32,
        precision=lax.Precision.HIGHEST,
    )


def blur_taps(half_width):
    offsets = (
        lax.broadcasted_iota(jnp.int32, (2 * half_width + 1,), 0).astype(jnp.float32) - half_width
    )
    weights = jnp.exp(-offsets * offsets / (2.0 * BLUR_SIGMA * BLUR_SIGMA))
    return weights / jnp.sum(weights)


def windows_last(padded, half_width):
    length = padded.shape[-1] - 2 * half_width
    blocks = length // 128
    pad_spec = [(0, 0)] * (padded.ndim - 1) + [(0, 128 - 2 * half_width)]
    spread = jnp.pad(padded, pad_spec).reshape(padded.shape[:-1] + (blocks + 1, 128))
    return jnp.concatenate([spread[..., :blocks, :], spread[..., 1:, : 2 * half_width]], axis=-1)


def windows_rows(padded, half_width):
    length = padded.shape[-2] - 2 * half_width
    blocks = length // 128
    pad_spec = [(0, 0)] * (padded.ndim - 2) + [(0, 128 - 2 * half_width), (0, 0)]
    spread = jnp.pad(padded, pad_spec).reshape(
        padded.shape[:-2] + (blocks + 1, 128, padded.shape[-1])
    )
    return jnp.concatenate(
        [spread[..., :blocks, :, :], spread[..., 1:, : 2 * half_width, :]], axis=-2
    )


def blur_straight(extended, blur_mat, half_width):
    sideways = jnp.einsum(
        "rbi,ij->rbj", windows_last(extended, half_width), blur_mat, precision=lax.Precision.HIGHEST
    )
    sideways = sideways.reshape(extended.shape[0], -1)
    downward = jnp.einsum(
        "biw,ij->bjw", windows_rows(sideways, half_width), blur_mat, precision=lax.Precision.HIGHEST
    )
    return downward.reshape(-1, sideways.shape[1])


def place_cells(library, cell_ids, cell_slots, cell_count, tile_rows, tile_cols, out_spec):
    cell_rows, cell_cols = (library.shape[1], library.shape[2])
    slot_rows = tile_rows // cell_rows
    slot_cols = tile_cols // cell_cols
    entries = cell_ids.shape[-1]
    ids_flat = cell_ids.reshape(entries)
    entry_iota = lax.broadcasted_iota(jnp.int32, (entries,), 0)
    is_live = entry_iota < cell_count.reshape(())
    slot_hit = (
        cell_slots.reshape(entries, 1)
        == lax.broadcasted_iota(jnp.int32, (1, slot_rows * slot_cols), 1)
    ) & is_live[:, None]
    slot_hit = slot_hit.astype(jnp.float32)
    sizes_by_letter = {"a": slot_rows, "p": cell_rows, "b": slot_cols, "q": cell_cols}
    empty_sum = jnp.zeros(tuple((sizes_by_letter[letter] for letter in out_spec)), jnp.float32)
    shard_cells = lax.all_gather(library, "col", axis=0, tiled=True)
    count_here = shard_cells.shape[0]
    id_match = (ids_flat[:, None] == lax.broadcasted_iota(jnp.int32, (1, count_here), 1)).astype(
        jnp.float32
    )
    place_table = (
        jnp.dot(slot_hit.T, id_match).reshape(slot_rows, slot_cols, count_here).astype(jnp.bfloat16)
    )
    return empty_sum + jnp.einsum(
        "abk,kpq->" + out_spec, place_table, shard_cells, preferred_element_type=jnp.float32
    )


def on_device(
    mask_pixels, across_taps, down_taps, kernel_weights, library, cell_ids, cell_slots, cell_count
):
    tile_rows, tile_cols = mask_pixels.shape
    half_width = (across_taps.shape[-1] - 1) // 2
    pixels = mask_pixels.astype(jnp.bfloat16)
    padded_mask = extended_2(pixels, (("col", 1),), half_width)
    first_mats = band_matrix(across_taps, half_width).astype(jnp.bfloat16)
    second_mats = band_matrix(down_taps, half_width).astype(jnp.bfloat16)
    blur_mat = band_matrix(blur_taps(BLUR_HALF), BLUR_HALF)
    tall_mask = extended_2(padded_mask, (("row", 0),), half_width)
    tall_windows = windows_last(tall_mask, half_width)
    tall_rows = tile_rows + 2 * half_width

    def kernel_step(running, inputs):
        first_mat, second_mat, weight = inputs
        pass_one = jnp.einsum(
            "rbi,pij->prbj", tall_windows, first_mat, preferred_element_type=jnp.float32
        )
        pass_one = pass_one.reshape(2, tall_rows, tile_cols).astype(jnp.bfloat16)
        pass_two = jnp.einsum(
            "pbiw,pij->pbjw",
            windows_rows(pass_one, half_width),
            second_mat,
            preferred_element_type=jnp.float32,
        )
        pass_two = pass_two.reshape(2, tile_rows, tile_cols)
        return (running + weight * jnp.sum(pass_two * pass_two, axis=0), None)

    start_total = jnp.zeros((tile_rows, tile_cols), jnp.float32)
    flat_image = lax.scan(kernel_step, start_total, (first_mats, second_mats, kernel_weights))[0]
    placed = place_cells(library, cell_ids, cell_slots, cell_count, tile_rows, tile_cols, "apbq")
    intensity = flat_image + placed.reshape(tile_rows, tile_cols)
    extended = extended_2(
        intensity.astype(jnp.bfloat16), (("row", 0), ("col", 1)), BLUR_HALF
    ).astype(intensity.dtype)
    return blur_straight(extended, blur_mat, BLUR_HALF)


def solution(mesh):
    placed = (
        P(("frames", "row"), "col"),
        P(),
        P(),
        P(),
        P("col", None, None),
        P(("frames", "row"), "col", None),
        P(("frames", "row"), "col", None),
        P(("frames", "row"), "col"),
    )
    return jax.shard_map(
        on_device,
        mesh=mesh,
        in_specs=placed,
        out_specs=P(("frames", "row"), "col"),
        check_vma=False,
    )
```

profile of v0, /device:TPU:1, one launch (start us, length us, event | category | flops | bytes accessed | tf_op | source)
XLA Modules:
  0.0 98.3 jit_solution(8133458689836300485)
XLA Ops:
  1.2 4.0 %collective-permute-start = (bf16[256,16]{1,0:T(8,128)(2,1)S(1)}, bf16[256,16]{1,0:T(8,128)(2,1)S(1)}, u32[]{:S(2)}, u32[]{:S(2)}) collective-permute-start(bf16[256,16]{1,0:T(8,128)(2,1)S(1)} %get-tuple-element.140), channel_id=1, source_target_pairs={{0,1},{1,2},{2,3},{4,5},{5,6},{6,7},{8,9},{9,10},{10,11},{12,13},{... | collective-permute-start | bytes 24584 | tf_op jit(solution)/shard_map/ppermute | solution.py:17
  5.2 1.3 %collective-permute-start.1 = (bf16[256,16]{1,0:T(8,128)(2,1)S(1)}, bf16[256,16]{1,0:T(8,128)(2,1)S(1)}, u32[]{:S(2)}, u32[]{:S(2)}) collective-permute-start(bf16[256,16]{1,0:T(8,128)(2,1)S(1)} %get-tuple-element.141), channel_id=1, source_target_pairs={{1,0},{2,1},{3,2},{5,4},{6,5},{7,6},{9,8},{10,9},{11,10},{13,12},{... | collective-permute-start | bytes 24584 | tf_op jit(solution)/shard_map/ppermute | solution.py:18
  6.5 1.4 %fusion.29 = bf16[12,2,160,128]{3,0,1,2:T(8,128)(2,1)S(1)} fusion(bf16[12,2,33]{2,1,0:T(2,128)(2,1)} %param.12), kind=kOutput, calls=%fused_computation.27 | convolution fusion | flops 34283520 | bytes 984624 | tf_op jit(solution)/shard_map/...t,ijt->...ij/dot_general | solution.py:30
  8.0 1.8 %fusion.26 = bf16[12,2,160,128]{3,0,1,2:T(8,128)(2,1)} fusion(bf16[12,2,33]{2,1,0:T(2,128)(2,1)S(1)} %copy-done.2), kind=kOutput, calls=%fused_computation.26 | convolution fusion | flops 34283520 | bytes 984624 | tf_op jit(solution)/shard_map/...t,ijt->...ij/dot_general | solution.py:30
  10.9 14.3 %all_gather.3 = bf16[32,64,128]{2,0,1:T(8,128)(2,1)S(1)} all-gather(bf16[8,64,128]{2,0,1:T(8,128)(2,1)S(1)} %copy.32), channel_id=1, replica_groups=mesh['frames'=2,'row'=4,'col'=4] {'col'}, dimensions={0}, use_global_device_ids=true | all-gather | bytes 655360 | tf_op jit(solution)/shard_map/all_gather | solution.py:93
  25.3 5.8 %collective-permute-start.2 = (bf16[16,544]{1,0:T(8,128)(2,1)S(1)}, bf16[16,544]{1,0:T(8,128)(2,1)S(1)}, u32[]{:S(2)}, u32[]{:S(2)}) collective-permute-start(bf16[16,544]{1,0:T(8,128)(2,1)S(1)} %get-tuple-element.134), channel_id=1, source_target_pairs={{0,4},{4,8},{8,12},{1,5},{5,9},{9,13},{2,6},{6,10},{10,14},{3,7},{... | collective-permute-start | bytes 52232 | tf_op jit(solution)/shard_map/ppermute | solution.py:17
  31.1 1.9 %collective-permute-start.3 = (bf16[16,544]{1,0:T(8,128)(2,1)S(1)}, bf16[16,544]{1,0:T(8,128)(2,1)S(1)}, u32[]{:S(2)}, u32[]{:S(2)}) collective-permute-start(bf16[16,544]{1,0:T(8,128)(2,1)S(1)} %get-tuple-element.135), channel_id=1, source_target_pairs={{4,0},{8,4},{12,8},{5,1},{9,5},{13,9},{6,2},{10,6},{14,10},{7,3},{... | collective-permute-start | bytes 52232 | tf_op jit(solution)/shard_map/ppermute | solution.py:18
  33.2 1.3 %copy.30 = bf16[12,2,160,128]{3,2,1,0:T(8,128)(2,1)} copy(bf16[12,2,160,128]{3,0,1,2:T(8,128)(2,1)S(1)} %fusion.29) | data formatting | bytes 1966080
  37.3 39.7 %while.13 = (s32[]{:T(128)}, f32[256,512]{1,0:T(8,128)S(1)}, f32[12]{0:T(128)S(1)}, bf16[12,2,160,128]{3,2,1,0:T(8,128)(2,1)}, bf16[12,2,160,128]{3,2,1,0:T(8,12...) while((s32[]{:T(128)}, f32[256,512]{1,0:T(8,128)S(1)}, ...), condition=%wide.region_3.4_spmd.clone, body=%wide.region_1.3_spmd.clone.sunk | while | flops 180649984 | bytes 8913533 | solution.py:136
  37.9 1.3 %fusion.88 = f32[128,2,512]{2,0,1:T(8,128)S(1)} fusion(bf16[2,2,32,512]{3,2,1,0:T(8,128)(2,1)S(1)} %slice.94, bf16[2,2,128,512]{3,2,1,0:T(8,128)(2,1)S(1)} %slice.95, bf16[12,2,160,128]{3,2,1,0:T(8,128)(2,1)} %get-tuple-element.200, s32[]{:T(128)} %get-tuple-element.188), kind=kOutput, calls=%fused_computation.2.clone.1 | convolution fusion | flops 85590016 | bytes 1262080 | tf_op jit(solution)/shard_map/while/body/eval_jaxpr/pbiw,pij->pbjw/dot_general | solution.py:126
  41.2 1.3 %fusion.88 = f32[128,2,512]{2,0,1:T(8,128)S(1)} fusion(bf16[2,2,32,512]{3,2,1,0:T(8,128)(2,1)S(1)} %slice.94, bf16[2,2,128,512]{3,2,1,0:T(8,128)(2,1)S(1)} %slice.95, bf16[12,2,160,128]{3,2,1,0:T(8,128)(2,1)} %get-tuple-element.200, s32[]{:T(128)} %get-tuple-element.188), kind=kOutput, calls=%fused_computation.2.clone.1 | convolution fusion | flops 85590016 | bytes 1262080 | tf_op jit(solution)/shard_map/while/body/eval_jaxpr/pbiw,pij->pbjw/dot_general | solution.py:126
  44.5 1.3 %fusion.88 = f32[128,2,512]{2,0,1:T(8,128)S(1)} fusion(bf16[2,2,32,512]{3,2,1,0:T(8,128)(2,1)S(1)} %slice.94, bf16[2,2,128,512]{3,2,1,0:T(8,128)(2,1)S(1)} %slice.95, bf16[12,2,160,128]{3,2,1,0:T(8,128)(2,1)} %get-tuple-element.200, s32[]{:T(128)} %get-tuple-element.188), kind=kOutput, calls=%fused_computation.2.clone.1 | convolution fusion | flops 85590016 | bytes 1262080 | tf_op jit(solution)/shard_map/while/body/eval_jaxpr/pbiw,pij->pbjw/dot_general | solution.py:126
  47.8 1.3 %fusion.88 = f32[128,2,512]{2,0,1:T(8,128)S(1)} fusion(bf16[2,2,32,512]{3,2,1,0:T(8,128)(2,1)S(1)} %slice.94, bf16[2,2,128,512]{3,2,1,0:T(8,128)(2,1)S(1)} %slice.95, bf16[12,2,160,128]{3,2,1,0:T(8,128)(2,1)} %get-tuple-element.200, s32[]{:T(128)} %get-tuple-element.188), kind=kOutput, calls=%fused_computation.2.clone.1 | convolution fusion | flops 85590016 | bytes 1262080 | tf_op jit(solution)/shard_map/while/body/eval_jaxpr/pbiw,pij->pbjw/dot_general | solution.py:126
  51.2 1.3 %fusion.88 = f32[128,2,512]{2,0,1:T(8,128)S(1)} fusion(bf16[2,2,32,512]{3,2,1,0:T(8,128)(2,1)S(1)} %slice.94, bf16[2,2,128,512]{3,2,1,0:T(8,128)(2,1)S(1)} %slice.95, bf16[12,2,160,128]{3,2,1,0:T(8,128)(2,1)} %get-tuple-element.200, s32[]{:T(128)} %get-tuple-element.188), kind=kOutput, calls=%fused_computation.2.clone.1 | convolution fusion | flops 85590016 | bytes 1262080 | tf_op jit(solution)/shard_map/while/body/eval_jaxpr/pbiw,pij->pbjw/dot_general | solution.py:126
  57.8 1.3 %fusion.88 = f32[128,2,512]{2,0,1:T(8,128)S(1)} fusion(bf16[2,2,32,512]{3,2,1,0:T(8,128)(2,1)S(1)} %slice.94, bf16[2,2,128,512]{3,2,1,0:T(8,128)(2,1)S(1)} %slice.95, bf16[12,2,160,128]{3,2,1,0:T(8,128)(2,1)} %get-tuple-element.200, s32[]{:T(128)} %get-tuple-element.188), kind=kOutput, calls=%fused_computation.2.clone.1 | convolution fusion | flops 85590016 | bytes 1262080 | tf_op jit(solution)/shard_map/while/body/eval_jaxpr/pbiw,pij->pbjw/dot_general | solution.py:126
  67.7 1.3 %fusion.88 = f32[128,2,512]{2,0,1:T(8,128)S(1)} fusion(bf16[2,2,32,512]{3,2,1,0:T(8,128)(2,1)S(1)} %slice.94, bf16[2,2,128,512]{3,2,1,0:T(8,128)(2,1)S(1)} %slice.95, bf16[12,2,160,128]{3,2,1,0:T(8,128)(2,1)} %get-tuple-element.200, s32[]{:T(128)} %get-tuple-element.188), kind=kOutput, calls=%fused_computation.2.clone.1 | convolution fusion | flops 85590016 | bytes 1262080 | tf_op jit(solution)/shard_map/while/body/eval_jaxpr/pbiw,pij->pbjw/dot_general | solution.py:126
  77.1 2.4 %collective-permute-start.4 = (bf16[8,512]{1,0:T(8,128)(2,1)S(1)}, bf16[8,512]{1,0:T(8,128)(2,1)S(1)}, u32[]{:S(2)}, u32[]{:S(2)}) collective-permute-start(bf16[8,512]{1,0:T(8,128)(2,1)S(1)} %get-tuple-element.138), channel_id=1, source_target_pairs={{0,4},{4,8},{8,12},{1,5},{5,9},{9,13},{2,6},{6,10},{10,14},{3,7},{... | collective-permute-start | bytes 24584 | tf_op jit(solution)/shard_map/ppermute | solution.py:17
  79.5 1.9 %collective-permute-start.5 = (bf16[8,512]{1,0:T(8,128)(2,1)S(1)}, bf16[8,512]{1,0:T(8,128)(2,1)S(1)}, u32[]{:S(2)}, u32[]{:S(2)}) collective-permute-start(bf16[8,512]{1,0:T(8,128)(2,1)S(1)} %get-tuple-element.139), channel_id=1, source_target_pairs={{4,0},{8,4},{12,8},{5,1},{9,5},{13,9},{6,2},{10,6},{14,10},{7,3},{... | collective-permute-start | bytes 24584 | tf_op jit(solution)/shard_map/ppermute | solution.py:18
  82.2 2.2 %collective-permute-done.5 = bf16[8,512]{1,0:T(8,128)(2,1)S(1)} collective-permute-done((bf16[8,512]{1,0:T(8,128)(2,1)S(1)}, bf16[8,512]{1,0:T(8,128)(2,1)S(1)}, u32[]{:S(2)}, u32[]{:S(2)}) %collective-permute-start.5) | collective-permute-done | bytes 8224 | tf_op jit(solution)/shard_map/ppermute | solution.py:18
  84.6 3.6 %collective-permute-start.6 = (bf16[272,8]{1,0:T(8,128)(2,1)S(1)}, bf16[272,8]{1,0:T(8,128)(2,1)S(1)}, u32[]{:S(2)}, u32[]{:S(2)}) collective-permute-start(bf16[272,8]{1,0:T(8,128)(2,1)S(1)} %get-tuple-element.136), channel_id=1, source_target_pairs={{0,1},{1,2},{2,3},{4,5},{5,6},{6,7},{8,9},{9,10},{10,11},{12,13},{... | collective-permute-start | bytes 13064 | tf_op jit(solution)/shard_map/ppermute | solution.py:17
  88.2 1.3 %collective-permute-start.7 = (bf16[272,8]{1,0:T(8,128)(2,1)S(1)}, bf16[272,8]{1,0:T(8,128)(2,1)S(1)}, u32[]{:S(2)}, u32[]{:S(2)}) collective-permute-start(bf16[272,8]{1,0:T(8,128)(2,1)S(1)} %get-tuple-element.137), channel_id=1, source_target_pairs={{1,0},{2,1},{3,2},{5,4},{6,5},{7,6},{9,8},{10,9},{11,10},{13,12},{... | collective-permute-start | bytes 13064 | tf_op jit(solution)/shard_map/ppermute | solution.py:18
  90.7 2.5 %collective-permute-done.7 = bf16[272,8]{1,0:T(8,128)(2,1)S(1)} collective-permute-done((bf16[272,8]{1,0:T(8,128)(2,1)S(1)}, bf16[272,8]{1,0:T(8,128)(2,1)S(1)}, u32[]{:S(2)}, u32[]{:S(2)}) %collective-permute-start.7) | collective-permute-done | bytes 4384 | tf_op jit(solution)/shard_map/ppermute | solution.py:18
  93.9 2.3 %fusion.32 = f32[272,4,128]{2,0,1:T(8,128)S(1)} fusion(f32[144,128,1]{1,0,2:T(8,128)S(1)} %bitcast.115, f32[272,4,16]{0,2,1:T(8,128)S(1)} %slice.85, f32[272,4,128]{0,2,1:T(8,128)S(1)} %slice.84), kind=kOutput, calls=%fused_computation.30 | convolution fusion | flops 240804864 | bytes 1257472 | tf_op jit(solution)/shard_map/rbi,ij->rbj/dot_general | solution.py:68
  96.9 1.4 %fusion.41 = f32[128,2,512]{2,0,1:T(8,128)} fusion(f32[144,128,1]{1,0,2:T(8,128)S(1)} %bitcast.116, f32[2,16,512]{2,1,0:T(8,128)S(1)} %slice.87, f32[2,128,512]{2,1,0:T(8,128)S(1)} %slice.72), kind=kOutput, calls=%fused_computation.40 | convolution fusion | flops 226639872 | bytes 1187840 | tf_op jit(solution)/shard_map/biw,ij->bjw/dot_general | solution.py:72
  (150 shorter events, 37.8 us)
Async XLA Ops:
  0.0 8.0 %copy-start.2 = (bf16[12,2,33]{2,1,0:T(2,128)(2,1)S(1)}, bf16[12,2,33]{2,1,0:T(2,128)(2,1)}, u32[]{:S(2)}) copy-start(bf16[12,2,33]{2,1,0:T(2,128)(2,1)} %param.11) | copy-start | bytes 4756
  1.2 24.0 %collective-permute-start = (bf16[256,16]{1,0:T(8,128)(2,1)S(1)}, bf16[256,16]{1,0:T(8,128)(2,1)S(1)}, u32[]{:S(2)}, u32[]{:S(2)}) collective-permute-start(bf16[256,16]{1,0:T(8,128)(2,1)S(1)} %get-tuple-element.140), channel_id=1, source_target_pairs={{0,1},{1,2},{2,3},{4,5},{5,6},{6,7},{8,9},{9,10},{10,11},{12,13},{... | collective-permute-start | bytes 24584 | tf_op jit(solution)/shard_map/ppermute | solution.py:17
  5.2 20.0 %collective-permute-start.1 = (bf16[256,16]{1,0:T(8,128)(2,1)S(1)}, bf16[256,16]{1,0:T(8,128)(2,1)S(1)}, u32[]{:S(2)}, u32[]{:S(2)}) collective-permute-start(bf16[256,16]{1,0:T(8,128)(2,1)S(1)} %get-tuple-element.141), channel_id=1, source_target_pairs={{1,0},{2,1},{3,2},{5,4},{6,5},{7,6},{9,8},{10,9},{11,10},{13,12},{... | collective-permute-start | bytes 24584 | tf_op jit(solution)/shard_map/ppermute | solution.py:18
  8.0 1.9 %copy-start.1 = (bf16[8,64,128]{2,1,0:T(8,128)(2,1)S(1)}, bf16[8,64,128]{2,1,0:T(8,128)(2,1)}, u32[]{:S(2)}) copy-start(bf16[8,64,128]{2,1,0:T(8,128)(2,1)} %param.14) | copy-start | bytes 393220
  8.0 2.6 %copy-start.3 = (s32[1,1,8]{2,1,0:T(1,128)S(1)}, s32[1,1,8]{2,1,0:T(1,128)}, u32[]{:S(2)}) copy-start(s32[1,1,8]{2,1,0:T(1,128)} %param.15) | copy-start | bytes 100
  8.0 2.6 %copy-start.4 = (s32[1,1,8]{2,1,0:T(1,128)S(1)}, s32[1,1,8]{2,1,0:T(1,128)}, u32[]{:S(2)}) copy-start(s32[1,1,8]{2,1,0:T(1,128)} %param.16) | copy-start | bytes 100
  25.3 9.7 %collective-permute-start.2 = (bf16[16,544]{1,0:T(8,128)(2,1)S(1)}, bf16[16,544]{1,0:T(8,128)(2,1)S(1)}, u32[]{:S(2)}, u32[]{:S(2)}) collective-permute-start(bf16[16,544]{1,0:T(8,128)(2,1)S(1)} %get-tuple-element.134), channel_id=1, source_target_pairs={{0,4},{4,8},{8,12},{1,5},{5,9},{9,13},{2,6},{6,10},{10,14},{3,7},{... | collective-permute-start | bytes 52232 | tf_op jit(solution)/shard_map/ppermute | solution.py:17
  31.1 5.1 %collective-permute-start.3 = (bf16[16,544]{1,0:T(8,128)(2,1)S(1)}, bf16[16,544]{1,0:T(8,128)(2,1)S(1)}, u32[]{:S(2)}, u32[]{:S(2)}) collective-permute-start(bf16[16,544]{1,0:T(8,128)(2,1)S(1)} %get-tuple-element.135), channel_id=1, source_target_pairs={{4,0},{8,4},{12,8},{5,1},{9,5},{13,9},{6,2},{10,6},{14,10},{7,3},{... | collective-permute-start | bytes 52232 | tf_op jit(solution)/shard_map/ppermute | solution.py:18
  33.2 1.3 %copy-start = (bf16[12,2,160,128]{3,0,1,2:T(8,128)(2,1)S(1)}, bf16[12,2,160,128]{3,0,1,2:T(8,128)(2,1)}, u32[]{:S(2)}) copy-start(bf16[12,2,160,128]{3,0,1,2:T(8,128)(2,1)} %fusion.26) | copy-start | bytes 2949124
  36.6 0.7 copy-start.5
  77.1 5.2 %collective-permute-start.4 = (bf16[8,512]{1,0:T(8,128)(2,1)S(1)}, bf16[8,512]{1,0:T(8,128)(2,1)S(1)}, u32[]{:S(2)}, u32[]{:S(2)}) collective-permute-start(bf16[8,512]{1,0:T(8,128)(2,1)S(1)} %get-tuple-element.138), channel_id=1, source_target_pairs={{0,4},{4,8},{8,12},{1,5},{5,9},{9,13},{2,6},{6,10},{10,14},{3,7},{... | collective-permute-start | bytes 24584 | tf_op jit(solution)/shard_map/ppermute | solution.py:17
  79.5 5.0 %collective-permute-start.5 = (bf16[8,512]{1,0:T(8,128)(2,1)S(1)}, bf16[8,512]{1,0:T(8,128)(2,1)S(1)}, u32[]{:S(2)}, u32[]{:S(2)}) collective-permute-start(bf16[8,512]{1,0:T(8,128)(2,1)S(1)} %get-tuple-element.139), channel_id=1, source_target_pairs={{4,0},{8,4},{12,8},{5,1},{9,5},{13,9},{6,2},{10,6},{14,10},{7,3},{... | collective-permute-start | bytes 24584 | tf_op jit(solution)/shard_map/ppermute | solution.py:18
  84.6 6.1 %collective-permute-start.6 = (bf16[272,8]{1,0:T(8,128)(2,1)S(1)}, bf16[272,8]{1,0:T(8,128)(2,1)S(1)}, u32[]{:S(2)}, u32[]{:S(2)}) collective-permute-start(bf16[272,8]{1,0:T(8,128)(2,1)S(1)} %get-tuple-element.136), channel_id=1, source_target_pairs={{0,1},{1,2},{2,3},{4,5},{5,6},{6,7},{8,9},{9,10},{10,11},{12,13},{... | collective-permute-start | bytes 13064 | tf_op jit(solution)/shard_map/ppermute | solution.py:17
  88.2 5.1 %collective-permute-start.7 = (bf16[272,8]{1,0:T(8,128)(2,1)S(1)}, bf16[272,8]{1,0:T(8,128)(2,1)S(1)}, u32[]{:S(2)}, u32[]{:S(2)}) collective-permute-start(bf16[272,8]{1,0:T(8,128)(2,1)S(1)} %get-tuple-element.137), channel_id=1, source_target_pairs={{1,0},{2,1},{3,2},{5,4},{6,5},{7,6},{9,8},{10,9},{11,10},{13,12},{... | collective-permute-start | bytes 13064 | tf_op jit(solution)/shard_map/ppermute | solution.py:18
where the time goes:
time: 99.3 us; the launch traced here: 98.3 us
  matrix products  28.8 us (29%)
  starting transfers between devices  22.3 us (22%)
  blocking collectives  14.3 us (14%)
  local copies, waits for them, and re-layouts  13.4 us (13%)
  other arithmetic  11.7 us (12%)
  waiting for transfers between devices  6.03 us (6%)
    ppermute x4, starting transfers between devices, extended_2(): before = lax.ppermute(last, axis, up)  15.8 us
    dot_general x12, matrix products, kernel_step(): jnp.einsum('pbiw,pij->pbjw', windows_rows(pass_one, half_width), second_m...  15.3 us
    all_gather x1, blocking collectives, place_cells(): shard_cells = lax.all_gather(library, 'col', axis=0, tiled=True)  14.3 us
    mul x12, other arithmetic, kernel_step(): return (running + weight * jnp.sum(pass_two * pass_two, axis=0), None)  7.17 us
    dynamic_slice x12, local copies, waits for them, and re-layouts, on_device(): lax.scan(kernel_step, start_total, (first_mats, second_mats, kernel_weigh...  7.1 us
    ppermute x4, starting transfers between devices, extended_2(): after = lax.ppermute(initial, axis, down)  6.43 us
    ppermute x4, waiting for transfers between devices, extended_2(): after = lax.ppermute(initial, axis, down)  6.02 us
    dot_general x12, matrix products, kernel_step(): jnp.einsum('rbi,pij->prbj', tall_windows, first_mat, preferred_element_ty...  4.82 us
  transfers between devices with their start and end apart: 8, of which 3 were waited for; matrix products, arithmetic and copies ran while one was open for 8% of the time, Pallas kernels for 0%

commit v1 on v0

--- a/solution.py
+++ b/solution.py
@@ -90,7 +90,12 @@
     slot_hit = slot_hit.astype(jnp.float32)
     sizes_by_letter = {"a": slot_rows, "p": cell_rows, "b": slot_cols, "q": cell_cols}
     empty_sum = jnp.zeros(tuple((sizes_by_letter[letter] for letter in out_spec)), jnp.float32)
-    shard_cells = lax.all_gather(library, "col", axis=0, tiled=True)
+    ring = [library]
+    for hop in range(3):
+        ring.append(lax.ppermute(ring[-1], "col", [(dev, (dev + 1) % 4) for dev in range(4)]))
+    shard_cells = jnp.roll(
+        jnp.concatenate(ring[::-1], axis=0), (lax.axis_index("col") + 1) * ring[0].shape[0], axis=0
+    )
     count_here = shard_cells.shape[0]
     id_match = (ids_flat[:, None] == lax.broadcasted_iota(jnp.int32, (1, count_here), 1)).astype(
         jnp.float32

time: 99.3 us -> 91.6 us (0.922)
  the two profiles are of different devices: /device:TPU:1 before, /device:TPU:10 now
where the time goes in v1:
time: 91.6 us; the launch traced here: 90.6 us
  matrix products  28.8 us (31%)
  starting transfers between devices  23.3 us (25%)
  local copies, waits for them, and re-layouts  15.4 us (17%)
  other arithmetic  11.5 us (13%)
  waiting for transfers between devices  9.63 us (11%)
  between operations  1.09 us (1%)
  loops' own time  0.98 us (1%)
    dot_general x12, matrix products, kernel_step(): jnp.einsum('pbiw,pij->pbjw', windows_rows(pass_one, half_width), second_m...  15.3 us
    ppermute x4, starting transfers between devices, extended_2(): after = lax.ppermute(initial, axis, down)  11.8 us
    ppermute x4, starting transfers between devices, extended_2(): before = lax.ppermute(last, axis, up)  9.73 us
    mul x12, other arithmetic, kernel_step(): return (running + weight * jnp.sum(pass_two * pass_two, axis=0), None)  6.98 us
    dynamic_slice x12, local copies, waits for them, and re-layouts, on_device(): lax.scan(kernel_step, start_total, (first_mats, second_mats, kernel_weigh...  6.7 us
    ppermute x4, waiting for transfers between devices, extended_2(): before = lax.ppermute(last, axis, up)  5.32 us
    dot_general x12, matrix products, kernel_step(): jnp.einsum('rbi,pij->prbj', tall_windows, first_mat, preferred_element_ty...  4.83 us
    unnamed x25, local copies, waits for them, and re-layouts  4.76 us
  transfers between devices with their start and end apart: 11, of which 3 were waited for; matrix products, arithmetic and copies ran while one was open for 53% of the time, Pallas kernels for 0%

profile of v1, /device:TPU:10, one launch (start us, length us, event | category | flops | bytes accessed | tf_op | source)
XLA Modules:
  0.0 90.6 jit_solution(10700771416921952576)
XLA Ops:
  1.2 2.4 %collective-permute-start.1 = (bf16[256,16]{1,0:T(8,128)(2,1)S(1)}, bf16[256,16]{1,0:T(8,128)(2,1)S(1)}, u32[]{:S(2)}, u32[]{:S(2)}) collective-permute-start(bf16[256,16]{1,0:T(8,128)(2,1)S(1)} %get-tuple-element.141), channel_id=1, source_target_pairs={{1,0},{2,1},{3,2},{5,4},{6,5},{7,6},{9,8},{10,9},{11,10},{13,12},{... | collective-permute-start | bytes 24584 | tf_op jit(solution)/shard_map/ppermute | solution.py:18
  3.6 3.5 %collective-permute-start = (bf16[256,16]{1,0:T(8,128)(2,1)S(1)}, bf16[256,16]{1,0:T(8,128)(2,1)S(1)}, u32[]{:S(2)}, u32[]{:S(2)}) collective-permute-start(bf16[256,16]{1,0:T(8,128)(2,1)S(1)} %get-tuple-element.140), channel_id=1, source_target_pairs={{0,1},{1,2},{2,3},{4,5},{5,6},{6,7},{8,9},{9,10},{10,11},{12,13},{... | collective-permute-start | bytes 24584 | tf_op jit(solution)/shard_map/ppermute | solution.py:17
  8.1 1.6 %collective-permute-start.4 = (bf16[8,64,128]{2,0,1:T(8,128)(2,1)S(1)}, bf16[8,64,128]{2,0,1:T(8,128)(2,1)S(1)}, u32[]{:S(2)}, u32[]{:S(2)}) collective-permute-start(bf16[8,64,128]{2,0,1:T(8,128)(2,1)S(1)} %copy.37), channel_id=1, source_target_pairs={{0,1},{1,2},{2,3},{3,0},{4,5},{5,6},{6,7},{7,4},{8,9},{9,10},{10,1... | collective-permute-start | bytes 393224 | tf_op jit(solution)/shard_map/ppermute | solution.py:95
  9.7 1.8 %fusion.29 = bf16[12,2,160,128]{3,0,1,2:T(8,128)(2,1)} fusion(bf16[12,2,33]{2,1,0:T(2,128)(2,1)S(1)} %copy-done.2), kind=kOutput, calls=%fused_computation.27 | convolution fusion | flops 34283520 | bytes 984624 | tf_op jit(solution)/shard_map/...t,ijt->...ij/dot_general | solution.py:30
  13.1 1.9 %collective-permute-start.3 = (bf16[16,544]{1,0:T(8,128)(2,1)S(1)}, bf16[16,544]{1,0:T(8,128)(2,1)S(1)}, u32[]{:S(2)}, u32[]{:S(2)}) collective-permute-start(bf16[16,544]{1,0:T(8,128)(2,1)S(1)} %get-tuple-element.135), channel_id=1, source_target_pairs={{4,0},{8,4},{12,8},{5,1},{9,5},{13,9},{6,2},{10,6},{14,10},{7,3},{... | collective-permute-start | bytes 52232 | tf_op jit(solution)/shard_map/ppermute | solution.py:18
  15.0 2.4 %collective-permute-start.2 = (bf16[16,544]{1,0:T(8,128)(2,1)S(1)}, bf16[16,544]{1,0:T(8,128)(2,1)S(1)}, u32[]{:S(2)}, u32[]{:S(2)}) collective-permute-start(bf16[16,544]{1,0:T(8,128)(2,1)S(1)} %get-tuple-element.134), channel_id=1, source_target_pairs={{0,4},{4,8},{8,12},{1,5},{5,9},{9,13},{2,6},{6,10},{10,14},{3,7},{... | collective-permute-start | bytes 52232 | tf_op jit(solution)/shard_map/ppermute | solution.py:17
  18.3 2.6 %copy.35 = bf16[12,2,160,128]{3,2,1,0:T(8,128)(2,1)} copy(bf16[12,2,160,128]{3,0,1,2:T(8,128)(2,1)} %fusion.29) | data formatting | bytes 1966080
  22.1 4.3 %collective-permute-done.5 = bf16[8,64,128]{2,0,1:T(8,128)(2,1)S(1)} collective-permute-done((bf16[8,64,128]{2,0,1:T(8,128)(2,1)S(1)}, bf16[8,64,128]{2,0,1:T(8,128)(2,1)S(1)}, u32[]{:S(2)}, u32[]{:S(2)}) %collective-permute-start.5) | collective-permute-done | bytes 131104 | tf_op jit(solution)/shard_map/ppermute | solution.py:95
  26.5 39.1 %while.13 = (s32[]{:T(128)}, f32[256,512]{1,0:T(8,128)S(1)}, f32[12]{0:T(128)S(1)}, bf16[12,2,160,128]{3,2,1,0:T(8,128)(2,1)}, bf16[12,2,160,128]{3,2,1,0:T(8,12...) while((s32[]{:T(128)}, f32[256,512]{1,0:T(8,128)S(1)}, ...), condition=%wide.region_3.4_spmd.clone, body=%wide.region_1.3_spmd.clone.sunk | while | flops 180649984 | bytes 8913033 | solution.py:141
  27.1 1.3 %fusion.89 = f32[128,2,512]{2,0,1:T(8,128)S(1)} fusion(bf16[2,2,32,512]{3,2,1,0:T(8,128)(2,1)S(1)} %slice.94, bf16[2,2,128,512]{3,2,1,0:T(8,128)(2,1)S(1)} %slice.95, bf16[12,2,160,128]{3,2,1,0:T(8,128)(2,1)} %get-tuple-element.200, s32[]{:T(128)S(6)} %copy.74), kind=kOutput, calls=%fused_computation.2.clone.1 | convolution fusion | flops 85590016 | bytes 1261572 | tf_op jit(solution)/shard_map/while/body/eval_jaxpr/pbiw,pij->pbjw/dot_general | solution.py:131
  33.6 1.3 %fusion.89 = f32[128,2,512]{2,0,1:T(8,128)S(1)} fusion(bf16[2,2,32,512]{3,2,1,0:T(8,128)(2,1)S(1)} %slice.94, bf16[2,2,128,512]{3,2,1,0:T(8,128)(2,1)S(1)} %slice.95, bf16[12,2,160,128]{3,2,1,0:T(8,128)(2,1)} %get-tuple-element.200, s32[]{:T(128)S(6)} %copy.74), kind=kOutput, calls=%fused_computation.2.clone.1 | convolution fusion | flops 85590016 | bytes 1261572 | tf_op jit(solution)/shard_map/while/body/eval_jaxpr/pbiw,pij->pbjw/dot_general | solution.py:131
  36.9 1.3 %fusion.89 = f32[128,2,512]{2,0,1:T(8,128)S(1)} fusion(bf16[2,2,32,512]{3,2,1,0:T(8,128)(2,1)S(1)} %slice.94, bf16[2,2,128,512]{3,2,1,0:T(8,128)(2,1)S(1)} %slice.95, bf16[12,2,160,128]{3,2,1,0:T(8,128)(2,1)} %get-tuple-element.200, s32[]{:T(128)S(6)} %copy.74), kind=kOutput, calls=%fused_computation.2.clone.1 | convolution fusion | flops 85590016 | bytes 1261572 | tf_op jit(solution)/shard_map/while/body/eval_jaxpr/pbiw,pij->pbjw/dot_general | solution.py:131
  46.7 1.3 %fusion.89 = f32[128,2,512]{2,0,1:T(8,128)S(1)} fusion(bf16[2,2,32,512]{3,2,1,0:T(8,128)(2,1)S(1)} %slice.94, bf16[2,2,128,512]{3,2,1,0:T(8,128)(2,1)S(1)} %slice.95, bf16[12,2,160,128]{3,2,1,0:T(8,128)(2,1)} %get-tuple-element.200, s32[]{:T(128)S(6)} %copy.74), kind=kOutput, calls=%fused_computation.2.clone.1 | convolution fusion | flops 85590016 | bytes 1261572 | tf_op jit(solution)/shard_map/while/body/eval_jaxpr/pbiw,pij->pbjw/dot_general | solution.py:131
  49.9 1.3 %fusion.89 = f32[128,2,512]{2,0,1:T(8,128)S(1)} fusion(bf16[2,2,32,512]{3,2,1,0:T(8,128)(2,1)S(1)} %slice.94, bf16[2,2,128,512]{3,2,1,0:T(8,128)(2,1)S(1)} %slice.95, bf16[12,2,160,128]{3,2,1,0:T(8,128)(2,1)} %get-tuple-element.200, s32[]{:T(128)S(6)} %copy.74), kind=kOutput, calls=%fused_computation.2.clone.1 | convolution fusion | flops 85590016 | bytes 1261572 | tf_op jit(solution)/shard_map/while/body/eval_jaxpr/pbiw,pij->pbjw/dot_general | solution.py:131
  59.7 1.3 %fusion.89 = f32[128,2,512]{2,0,1:T(8,128)S(1)} fusion(bf16[2,2,32,512]{3,2,1,0:T(8,128)(2,1)S(1)} %slice.94, bf16[2,2,128,512]{3,2,1,0:T(8,128)(2,1)S(1)} %slice.95, bf16[12,2,160,128]{3,2,1,0:T(8,128)(2,1)} %get-tuple-element.200, s32[]{:T(128)S(6)} %copy.74), kind=kOutput, calls=%fused_computation.2.clone.1 | convolution fusion | flops 85590016 | bytes 1261572 | tf_op jit(solution)/shard_map/while/body/eval_jaxpr/pbiw,pij->pbjw/dot_general | solution.py:131
  63.0 1.3 %fusion.89 = f32[128,2,512]{2,0,1:T(8,128)S(1)} fusion(bf16[2,2,32,512]{3,2,1,0:T(8,128)(2,1)S(1)} %slice.94, bf16[2,2,128,512]{3,2,1,0:T(8,128)(2,1)S(1)} %slice.95, bf16[12,2,160,128]{3,2,1,0:T(8,128)(2,1)} %get-tuple-element.200, s32[]{:T(128)S(6)} %copy.74), kind=kOutput, calls=%fused_computation.2.clone.1 | convolution fusion | flops 85590016 | bytes 1261572 | tf_op jit(solution)/shard_map/while/body/eval_jaxpr/pbiw,pij->pbjw/dot_general | solution.py:131
  66.8 3.3 %collective-permute-start.8 = (bf16[8,512]{1,0:T(8,128)(2,1)S(1)}, bf16[8,512]{1,0:T(8,128)(2,1)S(1)}, u32[]{:S(2)}, u32[]{:S(2)}) collective-permute-start(bf16[8,512]{1,0:T(8,128)(2,1)S(1)} %get-tuple-element.139), channel_id=1, source_target_pairs={{4,0},{8,4},{12,8},{5,1},{9,5},{13,9},{6,2},{10,6},{14,10},{7,3},{... | collective-permute-start | bytes 24584 | tf_op jit(solution)/shard_map/ppermute | solution.py:18
  70.1 1.9 %collective-permute-start.7 = (bf16[8,512]{1,0:T(8,128)(2,1)S(1)}, bf16[8,512]{1,0:T(8,128)(2,1)S(1)}, u32[]{:S(2)}, u32[]{:S(2)}) collective-permute-start(bf16[8,512]{1,0:T(8,128)(2,1)S(1)} %get-tuple-element.138), channel_id=1, source_target_pairs={{0,4},{4,8},{8,12},{1,5},{5,9},{9,13},{2,6},{6,10},{10,14},{3,7},{... | collective-permute-start | bytes 24584 | tf_op jit(solution)/shard_map/ppermute | solution.py:17
  72.8 2.2 %collective-permute-done.7 = bf16[8,512]{1,0:T(8,128)(2,1)S(1)} collective-permute-done((bf16[8,512]{1,0:T(8,128)(2,1)S(1)}, bf16[8,512]{1,0:T(8,128)(2,1)S(1)}, u32[]{:S(2)}, u32[]{:S(2)}) %collective-permute-start.7) | collective-permute-done | bytes 8224 | tf_op jit(solution)/shard_map/ppermute | solution.py:17
  75.2 4.2 %collective-permute-start.10 = (bf16[272,8]{1,0:T(8,128)(2,1)S(1)}, bf16[272,8]{1,0:T(8,128)(2,1)S(1)}, u32[]{:S(2)}, u32[]{:S(2)}) collective-permute-start(bf16[272,8]{1,0:T(8,128)(2,1)S(1)} %get-tuple-element.137), channel_id=1, source_target_pairs={{1,0},{2,1},{3,2},{5,4},{6,5},{7,6},{9,8},{10,9},{11,10},{13,12},{... | collective-permute-start | bytes 13064 | tf_op jit(solution)/shard_map/ppermute | solution.py:18
  79.3 1.9 %collective-permute-start.9 = (bf16[272,8]{1,0:T(8,128)(2,1)S(1)}, bf16[272,8]{1,0:T(8,128)(2,1)S(1)}, u32[]{:S(2)}, u32[]{:S(2)}) collective-permute-start(bf16[272,8]{1,0:T(8,128)(2,1)S(1)} %get-tuple-element.136), channel_id=1, source_target_pairs={{0,1},{1,2},{2,3},{4,5},{5,6},{6,7},{8,9},{9,10},{10,11},{12,13},{... | collective-permute-start | bytes 13064 | tf_op jit(solution)/shard_map/ppermute | solution.py:17
  82.5 3.1 %collective-permute-done.9 = bf16[272,8]{1,0:T(8,128)(2,1)S(1)} collective-permute-done((bf16[272,8]{1,0:T(8,128)(2,1)S(1)}, bf16[272,8]{1,0:T(8,128)(2,1)S(1)}, u32[]{:S(2)}, u32[]{:S(2)}) %collective-permute-start.9) | collective-permute-done | bytes 4384 | tf_op jit(solution)/shard_map/ppermute | solution.py:17
  86.2 2.3 %fusion.32 = f32[272,4,128]{2,0,1:T(8,128)S(1)} fusion(f32[144,128,1]{1,0,2:T(8,128)S(1)} %bitcast.116, f32[272,4,16]{0,2,1:T(8,128)S(1)} %slice.85, f32[272,4,128]{0,2,1:T(8,128)S(1)} %slice.84), kind=kOutput, calls=%fused_computation.31 | convolution fusion | flops 240804864 | bytes 1257472 | tf_op jit(solution)/shard_map/rbi,ij->rbj/dot_general | solution.py:68
  89.2 1.4 %fusion.41 = f32[128,2,512]{2,0,1:T(8,128)} fusion(f32[144,128,1]{1,0,2:T(8,128)S(1)} %bitcast.117, f32[2,16,512]{2,1,0:T(8,128)S(1)} %slice.87, f32[2,128,512]{2,1,0:T(8,128)S(1)} %slice.72), kind=kOutput, calls=%fused_computation.41 | convolution fusion | flops 226639872 | bytes 1187840 | tf_op jit(solution)/shard_map/biw,ij->bjw/dot_general | solution.py:72
  (166 shorter events, 38.7 us)
Async XLA Ops:
  0.0 9.7 %copy-start.2 = (bf16[12,2,33]{2,1,0:T(2,128)(2,1)S(1)}, bf16[12,2,33]{2,1,0:T(2,128)(2,1)}, u32[]{:S(2)}) copy-start(bf16[12,2,33]{2,1,0:T(2,128)(2,1)} %param.12) | copy-start | bytes 4756
  1.1 10.4 %copy-start.3 = (bf16[12,2,33]{2,1,0:T(2,128)(2,1)S(1)}, bf16[12,2,33]{2,1,0:T(2,128)(2,1)}, u32[]{:S(2)}) copy-start(bf16[12,2,33]{2,1,0:T(2,128)(2,1)} %param.11) | copy-start | bytes 4756
  1.2 11.8 %collective-permute-start.1 = (bf16[256,16]{1,0:T(8,128)(2,1)S(1)}, bf16[256,16]{1,0:T(8,128)(2,1)S(1)}, u32[]{:S(2)}, u32[]{:S(2)}) collective-permute-start(bf16[256,16]{1,0:T(8,128)(2,1)S(1)} %get-tuple-element.141), channel_id=1, source_target_pairs={{1,0},{2,1},{3,2},{5,4},{6,5},{7,6},{9,8},{10,9},{11,10},{13,12},{... | collective-permute-start | bytes 24584 | tf_op jit(solution)/shard_map/ppermute | solution.py:18
  3.6 9.4 %collective-permute-start = (bf16[256,16]{1,0:T(8,128)(2,1)S(1)}, bf16[256,16]{1,0:T(8,128)(2,1)S(1)}, u32[]{:S(2)}, u32[]{:S(2)}) collective-permute-start(bf16[256,16]{1,0:T(8,128)(2,1)S(1)} %get-tuple-element.140), channel_id=1, source_target_pairs={{0,1},{1,2},{2,3},{4,5},{5,6},{6,7},{8,9},{9,10},{10,11},{12,13},{... | collective-permute-start | bytes 24584 | tf_op jit(solution)/shard_map/ppermute | solution.py:17
  8.1 13.3 %collective-permute-start.4 = (bf16[8,64,128]{2,0,1:T(8,128)(2,1)S(1)}, bf16[8,64,128]{2,0,1:T(8,128)(2,1)S(1)}, u32[]{:S(2)}, u32[]{:S(2)}) collective-permute-start(bf16[8,64,128]{2,0,1:T(8,128)(2,1)S(1)} %copy.37), channel_id=1, source_target_pairs={{0,1},{1,2},{2,3},{3,0},{4,5},{5,6},{6,7},{7,4},{8,9},{9,10},{10,1... | collective-permute-start | bytes 393224 | tf_op jit(solution)/shard_map/ppermute | solution.py:95
  11.5 5.9 %copy-start.4 = (s32[1,1,8]{2,1,0:T(1,128)S(1)}, s32[1,1,8]{2,1,0:T(1,128)}, u32[]{:S(2)}) copy-start(s32[1,1,8]{2,1,0:T(1,128)} %param.15) | copy-start | bytes 100
  11.5 5.9 %copy-start.5 = (s32[1,1,8]{2,1,0:T(1,128)S(1)}, s32[1,1,8]{2,1,0:T(1,128)}, u32[]{:S(2)}) copy-start(s32[1,1,8]{2,1,0:T(1,128)} %param.16) | copy-start | bytes 100
  13.1 8.3 %collective-permute-start.3 = (bf16[16,544]{1,0:T(8,128)(2,1)S(1)}, bf16[16,544]{1,0:T(8,128)(2,1)S(1)}, u32[]{:S(2)}, u32[]{:S(2)}) collective-permute-start(bf16[16,544]{1,0:T(8,128)(2,1)S(1)} %get-tuple-element.135), channel_id=1, source_target_pairs={{4,0},{8,4},{12,8},{5,1},{9,5},{13,9},{6,2},{10,6},{14,10},{7,3},{... | collective-permute-start | bytes 52232 | tf_op jit(solution)/shard_map/ppermute | solution.py:18
  15.0 6.4 %collective-permute-start.2 = (bf16[16,544]{1,0:T(8,128)(2,1)S(1)}, bf16[16,544]{1,0:T(8,128)(2,1)S(1)}, u32[]{:S(2)}, u32[]{:S(2)}) collective-permute-start(bf16[16,544]{1,0:T(8,128)(2,1)S(1)} %get-tuple-element.134), channel_id=1, source_target_pairs={{0,4},{4,8},{8,12},{1,5},{5,9},{9,13},{2,6},{6,10},{10,14},{3,7},{... | collective-permute-start | bytes 52232 | tf_op jit(solution)/shard_map/ppermute | solution.py:17
  21.3 5.0 %collective-permute-start.5 = (bf16[8,64,128]{2,0,1:T(8,128)(2,1)S(1)}, bf16[8,64,128]{2,0,1:T(8,128)(2,1)S(1)}, u32[]{:S(2)}, u32[]{:S(2)}) collective-permute-start(bf16[8,64,128]{2,0,1:T(8,128)(2,1)S(1)} %collective-permute-done.4), channel_id=1, source_target_pairs={{0,1},{1,2},{2,3},{3,0},{4,5},{5,6},{6,7},{7,4},{8,9},{9,10},{10,1... | collective-permute-start | bytes 393224 | tf_op jit(solution)/shard_map/ppermute | solution.py:95
  21.8 4.6 %copy-start.6 = (f32[12]{0:T(128)S(1)}, f32[12]{0:T(128)}, u32[]{:S(2)}) copy-start(f32[12]{0:T(128)} %param.13) | copy-start | bytes 148
  26.3 39.3 %collective-permute-start.6 = (bf16[8,64,128]{2,0,1:T(8,128)(2,1)S(1)}, bf16[8,64,128]{2,0,1:T(8,128)(2,1)S(1)}, u32[]{:S(2)}, u32[]{:S(2)}) collective-permute-start(bf16[8,64,128]{2,0,1:T(8,128)(2,1)S(1)} %collective-permute-done.5), channel_id=1, source_target_pairs={{0,1},{1,2},{2,3},{3,0},{4,5},{5,6},{6,7},{7,4},{8,9},{9,10},{10,1... | collective-permute-start | bytes 393224 | tf_op jit(solution)/shard_map/ppermute | solution.py:95
  26.5 39.3 %copy-start = (bf16[8,64,128]{2,1,0:T(8,128)(2,1)S(1)}, bf16[8,64,128]{2,1,0:T(8,128)(2,1)}, u32[]{:S(2)}) copy-start(bf16[8,64,128]{2,1,0:T(8,128)(2,1)} %param.14) | copy-start | bytes 393220
  65.6 0.7 copy-start.1
  66.8 6.1 %collective-permute-start.8 = (bf16[8,512]{1,0:T(8,128)(2,1)S(1)}, bf16[8,512]{1,0:T(8,128)(2,1)S(1)}, u32[]{:S(2)}, u32[]{:S(2)}) collective-permute-start(bf16[8,512]{1,0:T(8,128)(2,1)S(1)} %get-tuple-element.139), channel_id=1, source_target_pairs={{4,0},{8,4},{12,8},{5,1},{9,5},{13,9},{6,2},{10,6},{14,10},{7,3},{... | collective-permute-start | bytes 24584 | tf_op jit(solution)/shard_map/ppermute | solution.py:18
  70.1 5.0 %collective-permute-start.7 = (bf16[8,512]{1,0:T(8,128)(2,1)S(1)}, bf16[8,512]{1,0:T(8,128)(2,1)S(1)}, u32[]{:S(2)}, u32[]{:S(2)}) collective-permute-start(bf16[8,512]{1,0:T(8,128)(2,1)S(1)} %get-tuple-element.138), channel_id=1, source_target_pairs={{0,4},{4,8},{8,12},{1,5},{5,9},{9,13},{2,6},{6,10},{10,14},{3,7},{... | collective-permute-start | bytes 24584 | tf_op jit(solution)/shard_map/ppermute | solution.py:17
  75.2 7.3 %collective-permute-start.10 = (bf16[272,8]{1,0:T(8,128)(2,1)S(1)}, bf16[272,8]{1,0:T(8,128)(2,1)S(1)}, u32[]{:S(2)}, u32[]{:S(2)}) collective-permute-start(bf16[272,8]{1,0:T(8,128)(2,1)S(1)} %get-tuple-element.137), channel_id=1, source_target_pairs={{1,0},{2,1},{3,2},{5,4},{6,5},{7,6},{9,8},{10,9},{11,10},{13,12},{... | collective-permute-start | bytes 13064 | tf_op jit(solution)/shard_map/ppermute | solution.py:18
  79.3 6.2 %collective-permute-start.9 = (bf16[272,8]{1,0:T(8,128)(2,1)S(1)}, bf16[272,8]{1,0:T(8,128)(2,1)S(1)}, u32[]{:S(2)}, u32[]{:S(2)}) collective-permute-start(bf16[272,8]{1,0:T(8,128)(2,1)S(1)} %get-tuple-element.136), channel_id=1, source_target_pairs={{0,1},{1,2},{2,3},{4,5},{5,6},{6,7},{8,9},{9,10},{10,11},{12,13},{... | collective-permute-start | bytes 13064 | tf_op jit(solution)/shard_map/ppermute | solution.py:17
